TPU v7x, 32 devices: a whole 2x2x4 slice. The times are simulated.
32 devices in a mesh: tm: 8 (over z, y), head: 4 (over x, core).
Axes of the slice: x: 2, y: 2, z: 4, core: 2. Of those that a mesh axis runs over, the one named last changes fastest.
Arguments:
- query: bfloat16 [1024, 2560], P('tm', 'head'), may hold values from -8 to 8
- key: bfloat16 [1024, 2560], P('tm', 'head'), may hold values from -8 to 8
- value: bfloat16 [1024, 2560], P('tm', 'head'), may hold values from -6 to 6
- grad_out: bfloat16 [1024, 2560], P('tm', 'head'), may hold values from -6 to 6
- frame_ids: int32 [8], replicated, may hold values from 0 to 2, as said below
- sink_frame: int32 [1], replicated, may hold values from 0 to 2
- window: int32 [20], P('head'), may hold values from 1 to 3, as said below
Outputs:
- attended: bfloat16 [1024, 2560], P('tm', 'head')
- query_grad: bfloat16 [1024, 2560], P('tm', 'head')
- key_grad: bfloat16 [1024, 2560], P('tm', 'head')
- value_grad: bfloat16 [1024, 2560], P('tm', 'head')
Inputs may be any that keep to these rules, and one draw needn't show every extreme that they name: frame_ids[b] = (b + c) // 4 for one c of 1 to 3: every frame is four blocks except the first and the last, which have 4 - c and c blocks. Some head has a window of 3 and some a window of 1.
All inputs are finite; a program needn't handle non-finite values.
Results may differ from a plain program's by a relative error of at most 0.033.
Values may be sent and summed in bfloat16 or wider, within the bound.
No kernel may reach another device: no remote copies, remote signals or barrier semaphores. Data moves between devices by JAX's collectives and lax.ppermute only.
A program may use at most 128 MiB of HBM per device.

v0:
```python
import functools
import math

import jax
import jax.numpy as jnp
import numpy as np
from jax import lax
from jax.experimental import pallas as pl
from jax.experimental.pallas import tpu as pltpu
from jax.sharding import PartitionSpec as P

hidden_score = -1e30
MIB = 1 << 20
vmem_bytes = 64 * MIB
split_limit = 1024


even_rounds = (
    {
        1: (4, 6, 3, 2, 7, 0, 5),
        2: (3, 7, 5, 6, 1, 4, 0),
        3: (2, 0, 4, 5, 6, 7, 1),
        4: (7, 3, 2, 1, 0, 5, 6),
        5: (1, 2, 6, 0, 4, 3, 7),
    },
    {
        0: (5, 7, 6, 3, 1, 2, 4),
        1: (6, 4, 5, 7, 2, 3, 0),
        4: (0, 1, 7, 2, 5, 6, 3),
        6: (2, 5, 1, 4, 3, 0, 7),
        7: (3, 2, 0, 1, 4, 5, 6),
    },
)
even_rounds_back = (2, 4, 5, 6, 7, 1, 3)


def plan(blocks, groups, heads):
    laid_out = []
    for group in range(groups):
        if blocks == 8 and heads == 5:
            laid_out.append(even_rounds[group % 2])
        else:
            owners = [(head * blocks // heads + group % 2) % blocks for head in range(heads)]
            laid_out.append({u: [(u - step) % blocks for step in range(1, blocks)] for u in owners})
    owned = np.full((groups, blocks), -1)
    sent = np.full((blocks, groups, blocks), -1)
    partner = np.full((blocks, groups, blocks), -1)
    pairs = [[] for _ in range(blocks)]
    for group, rounds in enumerate(laid_out):
        for head, (owner, sources) in enumerate(rounds.items()):
            owned[group, owner] = head
            for step, source in enumerate((owner, *sources)):
                sent[step, group, source] = head
                partner[step, group, owner] = source
                pairs[step].append((source * groups + group, owner * groups + group))
    return owned, sent, partner, [sorted(step) for step in pairs]


def looked_up(table, group, block):
    groups, blocks = table.shape
    period = next(p for p in range(1, groups + 1) if (table == table[np.arange(groups) % p]).all())
    bits = int(table.max() + 1).bit_length()
    per_word = 31 // bits
    word = jnp.int32(0)
    for row in range(period):
        for first in range(0, blocks, per_word):
            values = table[row, first : first + per_word] + 1
            packed = sum(int(value) << (bits * n) for n, value in enumerate(values))
            here = (lax.rem(group, period) == row) & (block >= first) & (block < first + per_word)
            word = jnp.where(here, packed, word)
    return ((word >> (bits * lax.rem(block, per_word))) & ((1 << bits) - 1)) - 1


def dot(a, b, contract):
    return lax.dot_general(a, b, (contract, ((), ())), preferred_element_type=jnp.float32)


NN = ((1,), (0,))
NT = ((1,), (1,))


def head_columns(head, width):
    return pl.ds(pl.multiple_of(head * width, width), width)


def pack_kernel(owned, partner, sent, width, query, key, value, grad_out, frame_ids, sink_frame, window, *refs):
    blocks = len(sent)
    home, outs, refs = refs[0], refs[1:blocks], refs[blocks:]
    staged, tiles, packed, frames_here, sink_here, window_here, in_sems, out_sems = refs
    group, block = lax.axis_index("head"), lax.axis_index("tm")
    arrays = (query, key, value, grad_out)
    loads = [pltpu.make_async_copy(a, staged.at[n], in_sems.at[n]) for n, a in enumerate(arrays)]
    small = ((frame_ids, frames_here), (sink_frame, sink_here), (window, window_here))
    loads += [pltpu.make_async_copy(a, here, in_sems.at[4 + n]) for n, (a, here) in enumerate(small)]
    for load in loads:
        load.start()
    heads = [looked_up(table, group, block) for table in sent]
    stores = [pltpu.make_async_copy(packed.at[n], out, out_sems.at[1 + n]) for n, out in enumerate(outs)]
    keep = pltpu.make_async_copy(tiles, home.at[pl.ds(0, tiles.shape[0])], out_sems.at[0])
    for load in loads:
        load.wait()

    def fill(target, head):
        columns = head_columns(head, width)
        for n in range(3):
            target[n] = staged[n, :, columns]
        target[3] = staged[3, :, columns].T

    for step, head in enumerate(heads[1:]):

        @pl.when(head >= 0)
        def _():
            fill(packed.at[step], head)
            stores[step].start()

    @pl.when(heads[0] >= 0)
    def _():
        fill(tiles, heads[0])
        if tiles.shape[0] > 4:
            frames = [frames_here[looked_up(table, group, block)] for table in partner]
            row = lax.broadcasted_iota(jnp.int32, tiles.shape[1:], 0)
            theirs, own = jnp.zeros_like(row), jnp.zeros_like(row)
            for n, frame in enumerate(frames):
                theirs = jnp.where(row // blocks == n, frame, theirs)
                own = jnp.where(lax.rem(row, blocks) == n, frame, own)
            tiles[4] = seen_bias(theirs, own, window_here[heads[0]], sink_here[0]).astype(tiles.dtype)
        keep.start()

    for step, head in enumerate(heads[1:]):

        @pl.when(head >= 0)
        def _():
            stores[step].wait()

    @pl.when(heads[0] >= 0)
    def _():
        keep.wait()


def unpack_kernel(sent, width, *refs):
    parts, (attended, query_grad, key_grad, value_grad) = refs[:-4], refs[-4:]
    group, block = lax.axis_index("head"), lax.axis_index("tm")
    for step, part in enumerate(parts):
        head = looked_up(sent[step], group, block)

        @pl.when(head >= 0)
        def _():
            columns = head_columns(head, width)
            attended[:, columns] = part[0].T
            query_grad[:, columns] = part[1].T
            key_grad[:, columns] = part[2]
            value_grad[:, columns] = part[3]


def head_kernel(owned, partner, rows, frame_ids, sink_frame, window, local, *refs):
    blocks = len(partner)
    parts, outs, scratch = refs[: blocks - 1], refs[blocks - 1 : 2 * blocks - 1], refs[2 * blocks - 1 :]
    (here, q_all, kt_all, vt_all, gt_all, weights, weights_low, grads_low, grad_scaled, dk, dv, res, sem) = scratch
    parts = (here, *parts)
    group, block = lax.axis_index("head"), lax.axis_index("tm")
    head = looked_up(owned, group, block)
    width = q_all.shape[1]
    scaling = 1.0 / math.sqrt(width)
    rescale = scaling * math.log2(math.e)
    stretch = weights.shape[1]
    half = stretch // 2
    each = half // rows

    @pl.when(head >= 0)
    def _():
        fetch = pltpu.make_async_copy(local.at[pl.ds(0, 4)], here, sem)
        fetch.start()
        span = window[head]
        sink = sink_frame[0]
        frames = [frame_ids[looked_up(table, group, block)] for table in partner]

        def placed(j):
            at = pl.ds(j * rows, rows)
            q_all[at, :] = parts[j][0]
            kt_all[:, at] = parts[j][1].T
            vt_all[:, at] = parts[j][2].T
            gt_all[:, at] = parts[j][3]

        for j in range(1, blocks):
            placed(j)
        fetch.wait()
        placed(0)
        dk[...] = jnp.zeros_like(dk)
        dv[...] = jnp.zeros_like(dv)
        lane_block = lax.broadcasted_iota(jnp.int32, (1, half), 1) // rows

        def one_stretch(i, carry):
            at = [pl.ds(pl.multiple_of(i * stretch + h * half, half), half) for h in range(2)]
            lanes = [pl.ds(h * half, half) for h in range(2)]
            keys = [pl.ds(j * rows, rows) for j in range(blocks)]
            q_rows = [q_all[at[h], :] for h in range(2)]
            top = [jnp.full((1, half), hidden_score, jnp.float32)] * 2
            total = [jnp.zeros((1, half), jnp.float32)] * 2
            delta = [None] * 2
            own = [[], []]
            for h in range(2):
                for k in range(each):
                    n = i * 2 * each + h * each + k
                    own[h].append(sum(jnp.where(n == j, frames[j], 0) for j in range(blocks)))

            def score(h, j):
                bias = jnp.zeros((1, half), jnp.float32)
                for k in range(each):
                    seen = (frames[j] <= own[h][k]) & (frames[j] > own[h][k] - span)
                    seen = seen | ((frames[j] == sink) & (sink <= own[h][k]))
                    bias = jnp.where(lane_block == k, jnp.where(seen, 0.0, hidden_score), bias)
                scores = dot(parts[j][1], q_rows[h], NT) * rescale + bias
                weights[keys[j], lanes[h]] = scores
                top[h] = jnp.maximum(top[h], jnp.max(scores, axis=0, keepdims=True))

            def weigh(h, j):
                p = jnp.exp2(weights[keys[j], lanes[h]] - top[h])
                total[h] = total[h] + jnp.sum(p, axis=0, keepdims=True)
                weights[keys[j], lanes[h]] = p
                weights_low[keys[j], lanes[h]] = p.astype(jnp.bfloat16)

            def attend(h):
                inverse = 1.0 / total[h]
                mixed = (dot(vt_all[...], weights_low[:, lanes[h]], NN) * inverse).astype(jnp.bfloat16)
                grad_t = gt_all[:, at[h]].astype(jnp.float32)
                delta[h] = jnp.sum(grad_t * mixed.astype(jnp.float32), axis=0, keepdims=True) * inverse
                grad_scaled[:, lanes[h]] = (grad_t * inverse).astype(jnp.bfloat16)
                for k in range(each):
                    res[i * 2 * each + h * each + k, 0] = mixed[:, k * rows : (k + 1) * rows]

            def differ(h, j):
                g = dot(parts[j][2], grad_scaled[:, lanes[h]], NN) - delta[h]
                grads_low[keys[j], lanes[h]] = (weights[keys[j], lanes[h]] * g).astype(jnp.bfloat16)

            def query_part(h):
                grad = (dot(kt_all[...], grads_low[:, lanes[h]], NN) * scaling).astype(jnp.bfloat16)
                for k in range(each):
                    res[i * 2 * each + h * each + k, 1] = grad[:, k * rows : (k + 1) * rows]

            for j in range(blocks):
                score(0, j)
            for j in range(blocks):
                score(1, j)
                weigh(0, j)
            attend(0)
            for j in range(blocks):
                weigh(1, j)
                differ(0, j)
            attend(1)
            query_part(0)
            q_both = jnp.concatenate(q_rows, axis=0)
            for j in range(blocks):
                differ(1, j)
                dk[keys[j], :] += dot(grads_low[keys[j], :], q_both, NN)
                dv[keys[j], :] += dot(weights_low[keys[j], :], grad_scaled[...], NT)
            query_part(1)
            return carry

        lax.fori_loop(0, blocks * rows // stretch, one_stretch, 0)
        for j, out in enumerate(outs):
            at = pl.ds(j * rows, rows)
            out[0] = res[j, 0]
            out[1] = res[j, 1]
            out[2] = (dk[at, :] * scaling).astype(jnp.bfloat16)
            out[3] = dv[at, :].astype(jnp.bfloat16)


def seen_bias(frame, own, span, sink):
    seen = ((frame <= own) & (frame > own - span)) | ((frame == sink) & (sink <= own))
    return jnp.where(seen, 0.0, hidden_score)


def frames_by_lane(frames, rows):
    lane_block = lax.broadcasted_iota(jnp.int32, (1, len(frames) * rows), 1) // rows
    row = jnp.zeros_like(lane_block)
    for n, frame in enumerate(frames):
        row = jnp.where(lane_block == n, frame, row)
    return row


def place_block(part, j, rows, q_all, k_all, v_all, kt_all, vt_all, gt_all):
    at = pl.ds(j * rows, rows)
    q_all[at, :] = part[0]
    k_all[at, :] = part[1]
    v_all[at, :] = part[2]
    kt_all[:, at] = part[1].T
    vt_all[:, at] = part[2].T
    gt_all[:, at] = part[3]


def pair_products(j, held, rows, bias, scores, dots, q_all, k_all, v_all, gt_all):
    width = q_all.shape[1]
    rescale = math.log2(math.e) / math.sqrt(width)
    before = held * rows
    at = pl.ds(j * rows, rows)
    every = pl.ds(0, before + rows)
    scores[at, every] = dot(k_all[at, :], q_all[every, :], NT) * rescale + bias[pl.ds(j, 1), every]
    dots[at, every] = dot(v_all[at, :], gt_all[:, every], NN)
    column = dot(k_all[pl.ds(0, before), :], q_all[at, :], NT) * rescale
    for n in range(held):
        keys = pl.ds(n * rows, rows)
        scores[keys, at] = column[n * rows : (n + 1) * rows, :] + bias[pl.ds(n, 1), at]
    dots[pl.ds(0, before), at] = dot(v_all[pl.ds(0, before), :], gt_all[:, at], NN)


def lane_chunks(start, stop, size):
    return [pl.ds(first, min(size, stop - first)) for first in range(start, stop, size)]


def products_kernel(owned, blocks, rows, home, *refs):
    held = blocks - 2
    parts, refs = refs[: held - 1], refs[held - 1 :]
    bias, scores, dots, *places, tiles, sem = refs
    head = looked_up(owned, lax.axis_index("head"), lax.axis_index("tm"))

    @pl.when(head >= 0)
    def _():
        fetch = pltpu.make_async_copy(home.at[pl.ds(0, tiles.shape[0])], tiles, sem)
        fetch.start()
        for j, part in enumerate(parts):
            place_block(part, j + 1, rows, *places)
        fetch.wait()
        place_block(tiles, 0, rows, *places)
        mask = tiles[4].astype(jnp.float32)
        for j in range(blocks):
            for n in range(blocks):
                row = j * blocks + n
                bias[pl.ds(j, 1), pl.ds(n * rows, rows)] = mask[row : row + 1, :]
        q_all, k_all, v_all, _, _, gt_all = places
        lanes = pl.ds(0, held * rows)
        rescale = math.log2(math.e) / math.sqrt(q_all.shape[1])
        for j in range(held):
            keys = pl.ds(j * rows, rows)
            scores[keys, lanes] = dot(k_all[keys, :], q_all[lanes, :], NT) * rescale + bias[pl.ds(j, 1), lanes]
            dots[keys, lanes] = dot(v_all[keys, :], gt_all[:, lanes], NN)


def softmax_kernel(owned, blocks, rows, bias, *refs):
    part, refs = refs[0], refs[9:]
    scores, dots, q_all, k_all, v_all, kt_all, vt_all, gt_all, low, stats, mixed = refs
    head = looked_up(owned, lax.axis_index("head"), lax.axis_index("tm"))

    @pl.when(head >= 0)
    def _():
        newest = blocks - 2
        held = pl.ds(0, (newest + 1) * rows)
        place_block(part, newest, rows, q_all, k_all, v_all, kt_all, vt_all, gt_all)
        pair_products(newest, newest, rows, bias, scores, dots, q_all, k_all, v_all, gt_all)
        for lanes in lane_chunks(0, (newest + 1) * rows, 2 * rows):
            top = jnp.max(scores[held, lanes], axis=0, keepdims=True)
            total = jnp.zeros_like(top)
            for j in range(newest + 1):
                keys = pl.ds(j * rows, rows)
                p = jnp.exp2(scores[keys, lanes] - top)
                total = total + jnp.sum(p, axis=0, keepdims=True)
                scores[keys, lanes] = p
                low[keys, lanes] = p.astype(jnp.bfloat16)
            stats[pl.ds(0, 1), lanes] = top
            stats[pl.ds(1, 1), lanes] = total
            mixed[:, lanes] = dot(vt_all[:, held], low[held, lanes], NN)


def finish_kernel(owned, blocks, rows, bias, stats, mixed, *refs):
    part, refs = refs[0], refs[10:]
    outs, refs = refs[:blocks], refs[blocks:]
    scores, dots, q_all, k_all, v_all, kt_all, vt_all, gt_all, low, grads_low, old_scaled, new_scaled, factors = refs
    head = looked_up(owned, lax.axis_index("head"), lax.axis_index("tm"))
    width = q_all.shape[1]
    scaling = 1.0 / math.sqrt(width)

    @pl.when(head >= 0)
    def _():
        newest = blocks - 1
        at = pl.ds(newest * rows, rows)
        place_block(part, newest, rows, q_all, k_all, v_all, kt_all, vt_all, gt_all)
        pair_products(newest, newest, rows, bias, scores, dots, q_all, k_all, v_all, gt_all)

        def settle(lanes, total, old_factor, weighted):
            inverse = 1.0 / total
            attended = (weighted * inverse).astype(jnp.bfloat16)
            grad_t = gt_all[:, lanes].astype(jnp.float32)
            delta = jnp.sum(grad_t * attended.astype(jnp.float32), axis=0, keepdims=True)
            old = inverse * old_factor
            old_scaled[:, lanes] = (grad_t * old).astype(jnp.bfloat16)
            new_scaled[:, lanes] = (grad_t * inverse).astype(jnp.bfloat16)
            factors[pl.ds(0, 1), lanes] = old
            factors[pl.ds(1, 1), lanes] = delta * old
            factors[pl.ds(2, 1), lanes] = inverse
            factors[pl.ds(3, 1), lanes] = delta * inverse
            for k in range(lanes.size // rows):
                outs[lanes.start // rows + k][0] = attended[:, k * rows : (k + 1) * rows]

        for lanes in lane_chunks(0, newest * rows, 2 * rows):
            fresh = scores[at, lanes]
            before = stats[pl.ds(0, 1), lanes]
            top = jnp.maximum(before, jnp.max(fresh, axis=0, keepdims=True))
            correction = jnp.exp2(before - top)
            p = jnp.exp2(fresh - top)
            p_low = p.astype(jnp.bfloat16)
            scores[at, lanes] = p
            low[at, lanes] = p_low
            total = stats[pl.ds(1, 1), lanes] * correction + jnp.sum(p, axis=0, keepdims=True)
            weighted = mixed[:, lanes] * correction + dot(vt_all[:, at], p_low, NN)
            settle(lanes, total, correction, weighted)
        column = scores[:, at]
        p = jnp.exp2(column - jnp.max(column, axis=0, keepdims=True))
        p_low = p.astype(jnp.bfloat16)
        scores[:, at] = p
        low[:, at] = p_low
        settle(at, jnp.sum(p, axis=0, keepdims=True), 1.0, dot(vt_all[...], p_low, NN))

        for j, out in enumerate(outs):
            keys = pl.ds(j * rows, rows)
            row = 0 if j < newest else 2
            scaled = old_scaled if j < newest else new_scaled
            for lanes in lane_chunks(0, blocks * rows, 4 * rows):
                g = dots[keys, lanes] * factors[pl.ds(row, 1), lanes] - factors[pl.ds(row + 1, 1), lanes]
                grads_low[keys, lanes] = (scores[keys, lanes] * g).astype(jnp.bfloat16)
            out[2] = (dot(grads_low[keys, :], q_all[...], NN) * scaling).astype(jnp.bfloat16)
            out[3] = dot(low[keys, :], scaled[...], NT).astype(jnp.bfloat16)
        for lanes in lane_chunks(0, blocks * rows, 2 * rows):
            grad = (dot(kt_all[...], grads_low[:, lanes], NN) * scaling).astype(jnp.bfloat16)
            for k in range(lanes.size // rows):
                outs[lanes.start // rows + k][1] = grad[:, k * rows : (k + 1) * rows]


def per_device(query, key, value, grad_out, frame_ids, sink_frame, window):
    rows, row_width = query.shape
    heads = window.shape[0]
    width = row_width // heads
    blocks = lax.axis_size("tm")
    owned, sent, partner, pairs = plan(blocks, lax.axis_size("head"), heads)
    axes = ("tm", "head")
    smem = pl.BlockSpec(memory_space=pltpu.SMEM)
    vmem = pl.BlockSpec(memory_space=pltpu.VMEM)
    in_place = pl.BlockSpec(memory_space=pltpu.HBM)
    part = jax.ShapeDtypeStruct((4, rows, width), query.dtype)
    local = jax.ShapeDtypeStruct(query.shape, query.dtype)

    tokens = blocks * rows
    split = tokens <= split_limit
    tiles = 5 if split else 4
    home_tiles = vmem_bytes // (2 * rows * width)
    home, *parts = pl.pallas_call(
        functools.partial(pack_kernel, owned, partner, sent, width),
        out_shape=[jax.ShapeDtypeStruct((home_tiles, rows, width), query.dtype)] + [part] * (blocks - 1),
        in_specs=[in_place] * 7,
        out_specs=[in_place] * blocks,
        scratch_shapes=[
            pltpu.VMEM((4, rows, row_width), query.dtype),
            pltpu.VMEM((tiles, rows, width), query.dtype),
            pltpu.VMEM((blocks - 1, 4, rows, width), query.dtype),
            pltpu.SMEM(frame_ids.shape, jnp.int32),
            pltpu.SMEM(sink_frame.shape, jnp.int32),
            pltpu.SMEM(window.shape, jnp.int32),
            pltpu.SemaphoreType.DMA((7,)),
            pltpu.SemaphoreType.DMA((blocks,)),
        ],
        compiler_params=pltpu.CompilerParams(vmem_limit_bytes=62 * MIB),
        name="pack",
    )(query, key, value, grad_out, frame_ids, sink_frame, window)
    parts = [lax.ppermute(parts[s - 1], axes, pairs[s]) for s in range(1, blocks)]

    stretch = (4 if blocks % 4 == 0 else 2) * rows
    low, full = query.dtype, jnp.float32
    if split:
        square = jax.ShapeDtypeStruct((tokens, tokens), full)
        tall = jax.ShapeDtypeStruct((tokens, width), low)
        wide = jax.ShapeDtypeStruct((width, tokens), low)
        table = jax.ShapeDtypeStruct((blocks, tokens), full)
        held = [square] * 2 + [tall] * 3 + [wide] * 3
        flops = 2 * rows * rows * width
        bias, *state = pl.pallas_call(
            functools.partial(products_kernel, owned, blocks, rows),
            out_shape=[table, *held],
            in_specs=[in_place] + [vmem] * (blocks - 3),
            out_specs=[vmem] * 9,
            scratch_shapes=[pltpu.VMEM((tiles, rows, width), low), pltpu.SemaphoreType.DMA],
            compiler_params=pltpu.CompilerParams(vmem_limit_bytes=20 * MIB),
            cost_estimate=pl.CostEstimate(
                flops=2 * flops * (blocks - 2) ** 2, bytes_accessed=8 * tokens * tokens, transcendentals=0
            ),
            name="products",
        )(home, *parts[:-2])
        *state, weights_low, stats, mixed = pl.pallas_call(
            functools.partial(softmax_kernel, owned, blocks, rows),
            out_shape=[
                *held,
                jax.ShapeDtypeStruct((tokens, tokens), low),
                table,
                jax.ShapeDtypeStruct((width, tokens), full),
            ],
            in_specs=[vmem] * 10,
            out_specs=[vmem] * 11,
            input_output_aliases={2 + n: n for n in range(8)},
            compiler_params=pltpu.CompilerParams(vmem_limit_bytes=20 * MIB),
            cost_estimate=pl.CostEstimate(
                flops=3 * flops * blocks**2, bytes_accessed=8 * tokens * tokens, transcendentals=tokens * tokens
            ),
            name="softmax",
        )(bias, parts[-2], *state)
        parts = pl.pallas_call(
            functools.partial(finish_kernel, owned, blocks, rows),
            out_shape=[part] * blocks + held + [jax.ShapeDtypeStruct((tokens, tokens), low)],
            in_specs=[vmem] * 13,
            out_specs=[vmem] * (blocks + 9),
            input_output_aliases={4 + n: blocks + n for n in range(9)},
            scratch_shapes=[
                pltpu.VMEM((tokens, tokens), low),
                pltpu.VMEM((width, tokens), low),
                pltpu.VMEM((width, tokens), low),
                pltpu.VMEM((8, tokens), full),
            ],
            compiler_params=pltpu.CompilerParams(vmem_limit_bytes=24 * MIB),
            name="finish",
        )(bias, stats, mixed, parts[-1], *state, weights_low)[:blocks]
    else:
        parts = pl.pallas_call(
            functools.partial(head_kernel, owned, partner, rows),
            out_shape=[part] * blocks,
            in_specs=[smem] * 3 + [pl.BlockSpec(memory_space=pl.ANY)] + [vmem] * (blocks - 1),
            out_specs=[vmem] * blocks,
            scratch_shapes=[
                pltpu.VMEM((4, rows, width), low),
                pltpu.VMEM((tokens, width), low),
                pltpu.VMEM((width, tokens), low),
                pltpu.VMEM((width, tokens), low),
                pltpu.VMEM((width, tokens), low),
                pltpu.VMEM((tokens, stretch), full),
                pltpu.VMEM((tokens, stretch), low),
                pltpu.VMEM((tokens, stretch), low),
                pltpu.VMEM((width, stretch), low),
                pltpu.VMEM((tokens, width), full),
                pltpu.VMEM((tokens, width), full),
                pltpu.VMEM((blocks, 2, width, rows), low),
                pltpu.SemaphoreType.DMA,
            ],
            compiler_params=pltpu.CompilerParams(vmem_limit_bytes=48 * MIB),
            name="head_attention",
        )(frame_ids, sink_frame, window, home, *parts)
    back = [[(owner, source) for source, owner in step] for step in pairs]
    order = even_rounds_back if blocks == 8 and heads == 5 else range(1, blocks)
    parts = [parts[0]] + [lax.ppermute(parts[s], axes, back[s]) for s in order]

    return pl.pallas_call(
        functools.partial(unpack_kernel, sent[np.array([0, *order])], width),
        out_shape=[local] * 4,
        in_specs=[vmem] * blocks,
        out_specs=[vmem] * 4,
        compiler_params=pltpu.CompilerParams(vmem_limit_bytes=24 * MIB),
        name="unpack",
    )(*parts)


def solution(mesh):
    spec = P("tm", "head")
    return jax.shard_map(
        per_device,
        mesh=mesh,
        in_specs=(spec, spec, spec, spec, P(), P(), P("head")),
        out_specs=(spec, spec, spec, spec),
        check_vma=False,
    )
```

profile of v0, /device:TPU:5, one launch (start us, length us, event | category | flops | bytes accessed | tf_op | source)
XLA Modules:
  0.0 58.1 jit_solution(9747979058185316323)
XLA Ops:
  1.3 2.4 %pack.1 = (bf16[2048,128,128]{2,1,0:T(8,128)(2,1)}, bf16[4,128,128]{2,1,0:T(8,128)(2,1)}, bf16[4,128,128]{2,1,0:T(8,128)(2,1)}, bf16[4,128,128]{2,1,0:T(8,128)(2...) custom-call(bf16[128,640]{1,0:T(8,128)(2,1)} %query.1, ...), custom_call_target="tpu_custom_call" | custom-call | tf_op jit(solution)/shard_map/pack/pallas_call | solution.py:444
  3.7 1.3 %collective-permute-start = (bf16[4,128,128]{2,1,0:T(8,128)(2,1)}, bf16[4,128,128]{2,1,0:T(8,128)(2,1)S(1)}, u32[]{:S(2)}, u32[]{:S(2)}) collective-permute-start(bf16[4,128,128]{2,1,0:T(8,128)(2,1)} %get-tuple-element.41), channel_id=1, source_target_pairs={{1,17},{3,19},{4,20},{6,22},{8,12},{9,25},{10,14},{11,27},{12,8},{... | collective-permute-start | bytes 393224 | tf_op jit(solution)/shard_map/ppermute | solution.py:462
  5.0 4.2 %collective-permute-start.1 = (bf16[4,128,128]{2,1,0:T(8,128)(2,1)}, bf16[4,128,128]{2,1,0:T(8,128)(2,1)S(1)}, u32[]{:S(2)}, u32[]{:S(2)}) collective-permute-start(bf16[4,128,128]{2,1,0:T(8,128)(2,1)} %get-tuple-element.42), channel_id=1, source_target_pairs={{0,12},{2,14},{5,17},{7,19},{8,20},{9,29},{10,22},{11,31},{12,16},... | collective-permute-start | bytes 393224 | tf_op jit(solution)/shard_map/ppermute | solution.py:462
  9.1 3.8 %collective-permute-start.2 = (bf16[4,128,128]{2,1,0:T(8,128)(2,1)}, bf16[4,128,128]{2,1,0:T(8,128)(2,1)S(1)}, u32[]{:S(2)}, u32[]{:S(2)}) collective-permute-start(bf16[4,128,128]{2,1,0:T(8,128)(2,1)} %get-tuple-element.43), channel_id=1, source_target_pairs={{1,29},{3,31},{5,25},{7,27},{8,16},{10,18},{12,4},{14,6},{16,12},{... | collective-permute-start | bytes 393224 | tf_op jit(solution)/shard_map/ppermute | solution.py:462
  13.0 3.9 %collective-permute-start.3 = (bf16[4,128,128]{2,1,0:T(8,128)(2,1)}, bf16[4,128,128]{2,1,0:T(8,128)(2,1)S(1)}, u32[]{:S(2)}, u32[]{:S(2)}) collective-permute-start(bf16[4,128,128]{2,1,0:T(8,128)(2,1)} %get-tuple-element.44), channel_id=1, source_target_pairs={{0,20},{2,22},{4,16},{5,29},{6,18},{7,31},{8,4},{9,17},{10,6},{11,... | collective-permute-start | bytes 393224 | tf_op jit(solution)/shard_map/ppermute | solution.py:462
  16.9 2.5 %collective-permute-start.4 = (bf16[4,128,128]{2,1,0:T(8,128)(2,1)}, bf16[4,128,128]{2,1,0:T(8,128)(2,1)S(1)}, u32[]{:S(2)}, u32[]{:S(2)}) collective-permute-start(bf16[4,128,128]{2,1,0:T(8,128)(2,1)} %get-tuple-element.45), channel_id=1, source_target_pairs={{0,16},{2,18},{4,8},{5,1},{6,10},{7,3},{9,5},{11,7},{13,25},{15,27... | collective-permute-start | bytes 393224 | tf_op jit(solution)/shard_map/ppermute | solution.py:462
  19.3 0.0 collective-permute-done.refs_0_
  19.3 1.3 %collective-permute-start.5 = (bf16[4,128,128]{2,1,0:T(8,128)(2,1)}, bf16[4,128,128]{2,1,0:T(8,128)(2,1)S(1)}, u32[]{:S(2)}, u32[]{:S(2)}) collective-permute-start(bf16[4,128,128]{2,1,0:T(8,128)(2,1)} %get-tuple-element.47), channel_id=1, source_target_pairs={{0,4},{1,25},{2,6},{3,27},{9,1},{11,3},{12,20},{13,5},{14,22},{15,... | collective-permute-start | bytes 393224 | tf_op jit(solution)/shard_map/ppermute | solution.py:462
  20.7 1.3 %collective-permute-start.6 = (bf16[4,128,128]{2,1,0:T(8,128)(2,1)}, bf16[4,128,128]{2,1,0:T(8,128)(2,1)S(1)}, u32[]{:S(2)}, u32[]{:S(2)}) collective-permute-start(bf16[4,128,128]{2,1,0:T(8,128)(2,1)} %get-tuple-element.58), channel_id=1, source_target_pairs={{0,8},{1,5},{2,10},{3,7},{4,12},{6,14},{13,17},{15,19},{17,1},{19,... | collective-permute-start | bytes 393224 | tf_op jit(solution)/shard_map/ppermute | solution.py:462
  22.0 0.0 collective-permute-done.2.refs_2_
  22.0 1.7 %collective-permute-done.4.refs_4_ = bf16[4,128,128]{2,1,0:T(8,128)(2,1)S(1)} collective-permute-done((bf16[4,128,128]{2,1,0:T(8,128)(2,1)}, bf16[4,128,128]{2,1,0:T(8,128)(2,1)S(1)}, u32[]{:S(2)}, u32[]{:S(2)}) %collective-permute-start.4) | collective-permute-done | bytes 131104 | tf_op jit(solution)/shard_map/ppermute | solution.py:462
  23.7 1.7 %products.1 = (f32[8,1024]{1,0:T(8,128)S(1)}, f32[1024,1024]{1,0:T(8,128)S(1)}, f32[1024,1024]{1,0:T(8,128)S(1)}, bf16[1024,128]{1,0:T(8,128)(2,1)S(1)}, bf16[10...) custom-call(bf16[2048,128,128]{2,1,0:T(8,128)(2,1)} %get-tuple-eleme, ...), custom_call_target="tpu_custom_call" | custom-call | flops 301989888 | bytes 8388608 | tf_op jit(solution)/shard_map/products/pallas_call | solution.py:473
  25.4 1.5 %softmax.1 = (f32[1024,1024]{1,0:T(8,128)S(1)}, f32[1024,1024]{1,0:T(8,128)S(1)}, bf16[1024,128]{1,0:T(8,128)(2,1)S(1)}, bf16[1024,128]{1,0:T(8,128)(2,1)S(1)}, ...) custom-call(f32[8,1024]{1,0:T(8,128)S(1)} %get-tuple-element.46.bias, ...), custom_call_target="tpu_custom_call", output_to_operand_aliasing={{0}: (2, {}), {1}: (3, {}), {2}: (4, {}), {3}: (5, {}), {4}... | custom-call | flops 805306368 | bytes 8388608 | tf_op jit(solution)/shard_map/softmax/pallas_call | solution.py:485
  27.0 0.9 %collective-permute-done.6.refs_0_ = bf16[4,128,128]{2,1,0:T(8,128)(2,1)S(1)} collective-permute-done((bf16[4,128,128]{2,1,0:T(8,128)(2,1)}, bf16[4,128,128]{2,1,0:T(8,128)(2,1)S(1)}, u32[]{:S(2)}, u32[]{:S(2)}) %collective-permute-start.6) | collective-permute-done | bytes 131104 | tf_op jit(solution)/shard_map/ppermute | solution.py:462
  27.8 2.5 %finish.1 = (bf16[4,128,128]{2,1,0:T(8,128)(2,1)S(1)}, bf16[4,128,128]{2,1,0:T(8,128)(2,1)S(1)}, bf16[4,128,128]{2,1,0:T(8,128)(2,1)S(1)}, bf16[4,128,128]{2,1,0...) custom-call(f32[8,1024]{1,0:T(8,128)S(1)} %get-tuple-element.46.bias, ...), custom_call_target="tpu_custom_call", output_to_operand_aliasing={{8}: (4, {}), {9}: (5, {}), {10}: (6, {}), {11}: (7, {}), {... | custom-call | tf_op jit(solution)/shard_map/finish/pallas_call | solution.py:502
  30.3 3.5 %collective-permute-start.7 = (bf16[4,128,128]{2,1,0:T(8,128)(2,1)S(1)}, bf16[4,128,128]{2,1,0:T(8,128)(2,1)S(1)}, u32[]{:S(2)}, u32[]{:S(2)}) collective-permute-start(bf16[4,128,128]{2,1,0:T(8,128)(2,1)S(1)} %get-tuple-element.69), channel_id=1, source_target_pairs={{12,0},{14,2},{17,5},{19,7},{20,8},{29,9},{22,10},{31,11},{16,12},... | collective-permute-start | bytes 393224 | tf_op jit(solution)/shard_map/ppermute | solution.py:543
  33.8 2.5 %collective-permute-start.8 = (bf16[4,128,128]{2,1,0:T(8,128)(2,1)S(1)}, bf16[4,128,128]{2,1,0:T(8,128)(2,1)S(1)}, u32[]{:S(2)}, u32[]{:S(2)}) collective-permute-start(bf16[4,128,128]{2,1,0:T(8,128)(2,1)S(1)} %get-tuple-element.70), channel_id=1, source_target_pairs={{20,0},{22,2},{16,4},{29,5},{18,6},{31,7},{4,8},{17,9},{6,10},{19,... | collective-permute-start | bytes 393224 | tf_op jit(solution)/shard_map/ppermute | solution.py:543
  36.3 1.9 %collective-permute-start.9 = (bf16[4,128,128]{2,1,0:T(8,128)(2,1)S(1)}, bf16[4,128,128]{2,1,0:T(8,128)(2,1)S(1)}, u32[]{:S(2)}, u32[]{:S(2)}) collective-permute-start(bf16[4,128,128]{2,1,0:T(8,128)(2,1)S(1)} %get-tuple-element.71), channel_id=1, source_target_pairs={{16,0},{18,2},{8,4},{1,5},{10,6},{3,7},{5,9},{7,11},{25,13},{27,15... | collective-permute-start | bytes 393224 | tf_op jit(solution)/shard_map/ppermute | solution.py:543
  38.2 1.3 %collective-permute-start.10 = (bf16[4,128,128]{2,1,0:T(8,128)(2,1)S(1)}, bf16[4,128,128]{2,1,0:T(8,128)(2,1)S(1)}, u32[]{:S(2)}, u32[]{:S(2)}) collective-permute-start(bf16[4,128,128]{2,1,0:T(8,128)(2,1)S(1)} %get-tuple-element.72), channel_id=1, source_target_pairs={{4,0},{25,1},{6,2},{27,3},{1,9},{3,11},{20,12},{5,13},{22,14},{7,1... | collective-permute-start | bytes 393224 | tf_op jit(solution)/shard_map/ppermute | solution.py:543
  39.5 4.0 %collective-permute-start.11 = (bf16[4,128,128]{2,1,0:T(8,128)(2,1)S(1)}, bf16[4,128,128]{2,1,0:T(8,128)(2,1)S(1)}, u32[]{:S(2)}, u32[]{:S(2)}) collective-permute-start(bf16[4,128,128]{2,1,0:T(8,128)(2,1)S(1)} %get-tuple-element.73), channel_id=1, source_target_pairs={{8,0},{5,1},{10,2},{7,3},{12,4},{14,6},{17,13},{19,15},{1,17},{3,1... | collective-permute-start | bytes 393224 | tf_op jit(solution)/shard_map/ppermute | solution.py:543
  43.5 4.9 %collective-permute-start.12 = (bf16[4,128,128]{2,1,0:T(8,128)(2,1)S(1)}, bf16[4,128,128]{2,1,0:T(8,128)(2,1)S(1)}, u32[]{:S(2)}, u32[]{:S(2)}) collective-permute-start(bf16[4,128,128]{2,1,0:T(8,128)(2,1)S(1)} %get-tuple-element.74), channel_id=1, source_target_pairs={{17,1},{19,3},{20,4},{22,6},{12,8},{25,9},{14,10},{27,11},{8,12},{... | collective-permute-start | bytes 393224 | tf_op jit(solution)/shard_map/ppermute | solution.py:543
  48.4 1.9 %collective-permute-start.13 = (bf16[4,128,128]{2,1,0:T(8,128)(2,1)S(1)}, bf16[4,128,128]{2,1,0:T(8,128)(2,1)S(1)}, u32[]{:S(2)}, u32[]{:S(2)}) collective-permute-start(bf16[4,128,128]{2,1,0:T(8,128)(2,1)S(1)} %get-tuple-element.75), channel_id=1, source_target_pairs={{29,1},{31,3},{25,5},{27,7},{16,8},{18,10},{4,12},{6,14},{12,16},{... | collective-permute-start | bytes 393224 | tf_op jit(solution)/shard_map/ppermute | solution.py:543
  50.4 6.4 %collective-permute-done.13.refs_7_ = bf16[4,128,128]{2,1,0:T(8,128)(2,1)S(1)} collective-permute-done((bf16[4,128,128]{2,1,0:T(8,128)(2,1)S(1)}, bf16[4,128,128]{2,1,0:T(8,128)(2,1)S(1)}, u32[]{:S(2)}, u32[]{:S(2)}) %collective-permute-start.13) | collective-permute-done | bytes 131104 | tf_op jit(solution)/shard_map/ppermute | solution.py:543
  56.9 1.2 %unpack.1 = (bf16[128,640]{1,0:T(8,128)(2,1)}, bf16[128,640]{1,0:T(8,128)(2,1)}, bf16[128,640]{1,0:T(8,128)(2,1)}, bf16[128,640]{1,0:T(8,128)(2,1)}) custom-call(bf16[4,128,128]{2,1,0:T(8,128)(2,1)S(1)} %get-tuple-element.68.refs_0_, bf16[4,128,128]{2,1,0:T(8,128)(2,1)S(1)} %collective-permute-done.7.refs_1_, ...), custom_call_target="tpu_custom_call" | custom-call | tf_op jit(solution)/shard_map/unpack/pallas_call | solution.py:545
  (9 shorter events, 0.0 us)
Async XLA Ops:
  3.7 15.7 %collective-permute-start = (bf16[4,128,128]{2,1,0:T(8,128)(2,1)}, bf16[4,128,128]{2,1,0:T(8,128)(2,1)S(1)}, u32[]{:S(2)}, u32[]{:S(2)}) collective-permute-start(bf16[4,128,128]{2,1,0:T(8,128)(2,1)} %get-tuple-element.41), channel_id=1, source_target_pairs={{1,17},{3,19},{4,20},{6,22},{8,12},{9,25},{10,14},{11,27},{12,8},{... | collective-permute-start | bytes 393224 | tf_op jit(solution)/shard_map/ppermute | solution.py:462
  5.0 15.7 %collective-permute-start.1 = (bf16[4,128,128]{2,1,0:T(8,128)(2,1)}, bf16[4,128,128]{2,1,0:T(8,128)(2,1)S(1)}, u32[]{:S(2)}, u32[]{:S(2)}) collective-permute-start(bf16[4,128,128]{2,1,0:T(8,128)(2,1)} %get-tuple-element.42), channel_id=1, source_target_pairs={{0,12},{2,14},{5,17},{7,19},{8,20},{9,29},{10,22},{11,31},{12,16},... | collective-permute-start | bytes 393224 | tf_op jit(solution)/shard_map/ppermute | solution.py:462
  9.1 12.8 %collective-permute-start.2 = (bf16[4,128,128]{2,1,0:T(8,128)(2,1)}, bf16[4,128,128]{2,1,0:T(8,128)(2,1)S(1)}, u32[]{:S(2)}, u32[]{:S(2)}) collective-permute-start(bf16[4,128,128]{2,1,0:T(8,128)(2,1)} %get-tuple-element.43), channel_id=1, source_target_pairs={{1,29},{3,31},{5,25},{7,27},{8,16},{10,18},{12,4},{14,6},{16,12},{... | collective-permute-start | bytes 393224 | tf_op jit(solution)/shard_map/ppermute | solution.py:462
  13.0 9.0 %collective-permute-start.3 = (bf16[4,128,128]{2,1,0:T(8,128)(2,1)}, bf16[4,128,128]{2,1,0:T(8,128)(2,1)S(1)}, u32[]{:S(2)}, u32[]{:S(2)}) collective-permute-start(bf16[4,128,128]{2,1,0:T(8,128)(2,1)} %get-tuple-element.44), channel_id=1, source_target_pairs={{0,20},{2,22},{4,16},{5,29},{6,18},{7,31},{8,4},{9,17},{10,6},{11,... | collective-permute-start | bytes 393224 | tf_op jit(solution)/shard_map/ppermute | solution.py:462
  16.9 6.8 %collective-permute-start.4 = (bf16[4,128,128]{2,1,0:T(8,128)(2,1)}, bf16[4,128,128]{2,1,0:T(8,128)(2,1)S(1)}, u32[]{:S(2)}, u32[]{:S(2)}) collective-permute-start(bf16[4,128,128]{2,1,0:T(8,128)(2,1)} %get-tuple-element.45), channel_id=1, source_target_pairs={{0,16},{2,18},{4,8},{5,1},{6,10},{7,3},{9,5},{11,7},{13,25},{15,27... | collective-permute-start | bytes 393224 | tf_op jit(solution)/shard_map/ppermute | solution.py:462
  19.3 6.1 %collective-permute-start.5 = (bf16[4,128,128]{2,1,0:T(8,128)(2,1)}, bf16[4,128,128]{2,1,0:T(8,128)(2,1)S(1)}, u32[]{:S(2)}, u32[]{:S(2)}) collective-permute-start(bf16[4,128,128]{2,1,0:T(8,128)(2,1)} %get-tuple-element.47), channel_id=1, source_target_pairs={{0,4},{1,25},{2,6},{3,27},{9,1},{11,3},{12,20},{13,5},{14,22},{15,... | collective-permute-start | bytes 393224 | tf_op jit(solution)/shard_map/ppermute | solution.py:462
  20.7 7.2 %collective-permute-start.6 = (bf16[4,128,128]{2,1,0:T(8,128)(2,1)}, bf16[4,128,128]{2,1,0:T(8,128)(2,1)S(1)}, u32[]{:S(2)}, u32[]{:S(2)}) collective-permute-start(bf16[4,128,128]{2,1,0:T(8,128)(2,1)} %get-tuple-element.58), channel_id=1, source_target_pairs={{0,8},{1,5},{2,10},{3,7},{4,12},{6,14},{13,17},{15,19},{17,1},{19,... | collective-permute-start | bytes 393224 | tf_op jit(solution)/shard_map/ppermute | solution.py:462
  30.3 13.2 %collective-permute-start.7 = (bf16[4,128,128]{2,1,0:T(8,128)(2,1)S(1)}, bf16[4,128,128]{2,1,0:T(8,128)(2,1)S(1)}, u32[]{:S(2)}, u32[]{:S(2)}) collective-permute-start(bf16[4,128,128]{2,1,0:T(8,128)(2,1)S(1)} %get-tuple-element.69), channel_id=1, source_target_pairs={{12,0},{14,2},{17,5},{19,7},{20,8},{29,9},{22,10},{31,11},{16,12},... | collective-permute-start | bytes 393224 | tf_op jit(solution)/shard_map/ppermute | solution.py:543
  33.8 14.6 %collective-permute-start.8 = (bf16[4,128,128]{2,1,0:T(8,128)(2,1)S(1)}, bf16[4,128,128]{2,1,0:T(8,128)(2,1)S(1)}, u32[]{:S(2)}, u32[]{:S(2)}) collective-permute-start(bf16[4,128,128]{2,1,0:T(8,128)(2,1)S(1)} %get-tuple-element.70), channel_id=1, source_target_pairs={{20,0},{22,2},{16,4},{29,5},{18,6},{31,7},{4,8},{17,9},{6,10},{19,... | collective-permute-start | bytes 393224 | tf_op jit(solution)/shard_map/ppermute | solution.py:543
  36.3 14.1 %collective-permute-start.9 = (bf16[4,128,128]{2,1,0:T(8,128)(2,1)S(1)}, bf16[4,128,128]{2,1,0:T(8,128)(2,1)S(1)}, u32[]{:S(2)}, u32[]{:S(2)}) collective-permute-start(bf16[4,128,128]{2,1,0:T(8,128)(2,1)S(1)} %get-tuple-element.71), channel_id=1, source_target_pairs={{16,0},{18,2},{8,4},{1,5},{10,6},{3,7},{5,9},{7,11},{25,13},{27,15... | collective-permute-start | bytes 393224 | tf_op jit(solution)/shard_map/ppermute | solution.py:543
  38.2 12.2 %collective-permute-start.10 = (bf16[4,128,128]{2,1,0:T(8,128)(2,1)S(1)}, bf16[4,128,128]{2,1,0:T(8,128)(2,1)S(1)}, u32[]{:S(2)}, u32[]{:S(2)}) collective-permute-start(bf16[4,128,128]{2,1,0:T(8,128)(2,1)S(1)} %get-tuple-element.72), channel_id=1, source_target_pairs={{4,0},{25,1},{6,2},{27,3},{1,9},{3,11},{20,12},{5,13},{22,14},{7,1... | collective-permute-start | bytes 393224 | tf_op jit(solution)/shard_map/ppermute | solution.py:543
  39.5 10.9 %collective-permute-start.11 = (bf16[4,128,128]{2,1,0:T(8,128)(2,1)S(1)}, bf16[4,128,128]{2,1,0:T(8,128)(2,1)S(1)}, u32[]{:S(2)}, u32[]{:S(2)}) collective-permute-start(bf16[4,128,128]{2,1,0:T(8,128)(2,1)S(1)} %get-tuple-element.73), channel_id=1, source_target_pairs={{8,0},{5,1},{10,2},{7,3},{12,4},{14,6},{17,13},{19,15},{1,17},{3,1... | collective-permute-start | bytes 393224 | tf_op jit(solution)/shard_map/ppermute | solution.py:543
  43.5 6.9 %collective-permute-start.12 = (bf16[4,128,128]{2,1,0:T(8,128)(2,1)S(1)}, bf16[4,128,128]{2,1,0:T(8,128)(2,1)S(1)}, u32[]{:S(2)}, u32[]{:S(2)}) collective-permute-start(bf16[4,128,128]{2,1,0:T(8,128)(2,1)S(1)} %get-tuple-element.74), channel_id=1, source_target_pairs={{17,1},{19,3},{20,4},{22,6},{12,8},{25,9},{14,10},{27,11},{8,12},{... | collective-permute-start | bytes 393224 | tf_op jit(solution)/shard_map/ppermute | solution.py:543
  48.4 8.4 %collective-permute-start.13 = (bf16[4,128,128]{2,1,0:T(8,128)(2,1)S(1)}, bf16[4,128,128]{2,1,0:T(8,128)(2,1)S(1)}, u32[]{:S(2)}, u32[]{:S(2)}) collective-permute-start(bf16[4,128,128]{2,1,0:T(8,128)(2,1)S(1)} %get-tuple-element.75), channel_id=1, source_target_pairs={{29,1},{31,3},{25,5},{27,7},{16,8},{18,10},{4,12},{6,14},{12,16},{... | collective-permute-start | bytes 393224 | tf_op jit(solution)/shard_map/ppermute | solution.py:543
where the time goes:
time: 58.5 us; the launch traced here: 58.1 us
  starting transfers between devices  38.2 us (65%)
  Pallas kernels  9.33 us (16%)
  waiting for transfers between devices  9.07 us (16%)
  between operations  1.51 us (3%)
    ppermute x7, starting transfers between devices, per_device(): parts = [parts[0]] + [lax.ppermute(parts[s], axes, back[s]) for s in order]  20 us
    ppermute x7, starting transfers between devices, per_device(): lax.ppermute(parts[s - 1], axes, pairs[s])  18.2 us
    ppermute x7, waiting for transfers between devices, per_device(): parts = [parts[0]] + [lax.ppermute(parts[s], axes, back[s]) for s in order]  6.45 us
    ppermute x7, waiting for transfers between devices, per_device(): lax.ppermute(parts[s - 1], axes, pairs[s])  2.61 us
    pallas_call x1, Pallas kernels, per_device(): pl.pallas_call(functools.partial(finish_kernel, owned, blocks, rows), out...  2.48 us
    pallas_call x1, Pallas kernels, per_device(): pl.pallas_call(functools.partial(pack_kernel, owned, partner, sent, width...  2.39 us
    pallas_call x1, Pallas kernels, per_device(): pl.pallas_call(functools.partial(products_kernel, owned, blocks, rows), o...  1.72 us
    pallas_call x1, Pallas kernels, per_device(): pl.pallas_call(functools.partial(softmax_kernel, owned, blocks, rows), ou...  1.52 us
  transfers between devices with their start and end apart: 14, of which 3 were waited for; matrix products, arithmetic and copies ran while one was open for 0% of the time, Pallas kernels for 6%

commit v1 on v0

--- a/solution.py
+++ b/solution.py
@@ -308,7 +308,7 @@
 
 
 def products_kernel(owned, blocks, rows, home, *refs):
-    held = blocks - 2
+    held = blocks - 3
     parts, refs = refs[: held - 1], refs[held - 1 :]
     bias, scores, dots, *places, tiles, sem = refs
     head = looked_up(owned, lax.axis_index("head"), lax.axis_index("tm"))
@@ -333,6 +333,16 @@
             keys = pl.ds(j * rows, rows)
             scores[keys, lanes] = dot(k_all[keys, :], q_all[lanes, :], NT) * rescale + bias[pl.ds(j, 1), lanes]
             dots[keys, lanes] = dot(v_all[keys, :], gt_all[:, lanes], NN)
+
+
+def join_kernel(owned, index, rows, bias, *refs):
+    part, (scores, dots, q_all, k_all, v_all, kt_all, vt_all, gt_all) = refs[0], refs[9:]
+    head = looked_up(owned, lax.axis_index("head"), lax.axis_index("tm"))
+
+    @pl.when(head >= 0)
+    def _():
+        place_block(part, index, rows, q_all, k_all, v_all, kt_all, vt_all, gt_all)
+        pair_products(index, index, rows, bias, scores, dots, q_all, k_all, v_all, gt_all)
 
 
 def softmax_kernel(owned, blocks, rows, bias, *refs):
@@ -473,15 +483,27 @@
         bias, *state = pl.pallas_call(
             functools.partial(products_kernel, owned, blocks, rows),
             out_shape=[table, *held],
-            in_specs=[in_place] + [vmem] * (blocks - 3),
+            in_specs=[in_place] + [vmem] * (blocks - 4),
             out_specs=[vmem] * 9,
             scratch_shapes=[pltpu.VMEM((tiles, rows, width), low), pltpu.SemaphoreType.DMA],
             compiler_params=pltpu.CompilerParams(vmem_limit_bytes=20 * MIB),
             cost_estimate=pl.CostEstimate(
-                flops=2 * flops * (blocks - 2) ** 2, bytes_accessed=8 * tokens * tokens, transcendentals=0
+                flops=2 * flops * (blocks - 3) ** 2, bytes_accessed=8 * tokens * tokens, transcendentals=0
             ),
             name="products",
-        )(home, *parts[:-2])
+        )(home, *parts[:-3])
+        state = pl.pallas_call(
+            functools.partial(join_kernel, owned, blocks - 3, rows),
+            out_shape=held,
+            in_specs=[vmem] * 10,
+            out_specs=[vmem] * 8,
+            input_output_aliases={2 + n: n for n in range(8)},
+            compiler_params=pltpu.CompilerParams(vmem_limit_bytes=20 * MIB),
+            cost_estimate=pl.CostEstimate(
+                flops=4 * flops * blocks, bytes_accessed=16 * tokens * rows, transcendentals=0
+            ),
+            name="join",
+        )(bias, parts[-3], *state)
         *state, weights_low, stats, mixed = pl.pallas_call(
             functools.partial(softmax_kernel, owned, blocks, rows),
             out_shape=[

time: 58.5 us -> 58.8 us (level)
  the two profiles are of different devices: /device:TPU:5 before, /device:TPU:7 now
where the time goes in v1:
time: 58.8 us; the launch traced here: 58.3 us
  starting transfers between devices  38.4 us (65%)
  Pallas kernels  9.55 us (16%)
  waiting for transfers between devices  8.85 us (15%)
  between operations  1.5 us (3%)
    ppermute x7, starting transfers between devices, per_device(): parts = [parts[0]] + [lax.ppermute(parts[s], axes, back[s]) for s in order]  20.2 us
    ppermute x7, starting transfers between devices, per_device(): lax.ppermute(parts[s - 1], axes, pairs[s])  18.2 us
    ppermute x7, waiting for transfers between devices, per_device(): parts = [parts[0]] + [lax.ppermute(parts[s], axes, back[s]) for s in order]  6.46 us
    pallas_call x1, Pallas kernels, per_device(): pl.pallas_call(functools.partial(finish_kernel, owned, blocks, rows), out...  2.48 us
    pallas_call x1, Pallas kernels, per_device(): pl.pallas_call(functools.partial(pack_kernel, owned, partner, sent, width...  2.39 us
    ppermute x7, waiting for transfers between devices, per_device(): lax.ppermute(parts[s - 1], axes, pairs[s])  2.38 us
    pallas_call x1, Pallas kernels, per_device(): pl.pallas_call(functools.partial(products_kernel, owned, blocks, rows), o...  1.61 us
    pallas_call x1, Pallas kernels, per_device(): pl.pallas_call(functools.partial(softmax_kernel, owned, blocks, rows), ou...  1.49 us
  transfers between devices with their start and end apart: 14, of which 5 were waited for; matrix products, arithmetic and copies ran while one was open for 0% of the time, Pallas kernels for 6%

profile of v1, /device:TPU:7, one launch (start us, length us, event | category | flops | bytes accessed | tf_op | source)
XLA Modules:
  0.0 58.3 jit_solution(8128697499794427476)
XLA Ops:
  1.3 2.4 %pack.1 = (bf16[2048,128,128]{2,1,0:T(8,128)(2,1)}, bf16[4,128,128]{2,1,0:T(8,128)(2,1)}, bf16[4,128,128]{2,1,0:T(8,128)(2,1)}, bf16[4,128,128]{2,1,0:T(8,128)(2...) custom-call(bf16[128,640]{1,0:T(8,128)(2,1)} %query.1, ...), custom_call_target="tpu_custom_call" | custom-call | tf_op jit(solution)/shard_map/pack/pallas_call | solution.py:454
  3.7 1.3 %collective-permute-start = (bf16[4,128,128]{2,1,0:T(8,128)(2,1)}, bf16[4,128,128]{2,1,0:T(8,128)(2,1)S(1)}, u32[]{:S(2)}, u32[]{:S(2)}) collective-permute-start(bf16[4,128,128]{2,1,0:T(8,128)(2,1)} %get-tuple-element.49), channel_id=1, source_target_pairs={{1,17},{3,19},{4,20},{6,22},{8,12},{9,25},{10,14},{11,27},{12,8},{... | collective-permute-start | bytes 393224 | tf_op jit(solution)/shard_map/ppermute | solution.py:472
  5.0 4.2 %collective-permute-start.1 = (bf16[4,128,128]{2,1,0:T(8,128)(2,1)}, bf16[4,128,128]{2,1,0:T(8,128)(2,1)S(1)}, u32[]{:S(2)}, u32[]{:S(2)}) collective-permute-start(bf16[4,128,128]{2,1,0:T(8,128)(2,1)} %get-tuple-element.50), channel_id=1, source_target_pairs={{0,12},{2,14},{5,17},{7,19},{8,20},{9,29},{10,22},{11,31},{12,16},... | collective-permute-start | bytes 393224 | tf_op jit(solution)/shard_map/ppermute | solution.py:472
  9.1 3.8 %collective-permute-start.2 = (bf16[4,128,128]{2,1,0:T(8,128)(2,1)}, bf16[4,128,128]{2,1,0:T(8,128)(2,1)S(1)}, u32[]{:S(2)}, u32[]{:S(2)}) collective-permute-start(bf16[4,128,128]{2,1,0:T(8,128)(2,1)} %get-tuple-element.51), channel_id=1, source_target_pairs={{1,29},{3,31},{5,25},{7,27},{8,16},{10,18},{12,4},{14,6},{16,12},{... | collective-permute-start | bytes 393224 | tf_op jit(solution)/shard_map/ppermute | solution.py:472
  13.0 3.9 %collective-permute-start.3 = (bf16[4,128,128]{2,1,0:T(8,128)(2,1)}, bf16[4,128,128]{2,1,0:T(8,128)(2,1)S(1)}, u32[]{:S(2)}, u32[]{:S(2)}) collective-permute-start(bf16[4,128,128]{2,1,0:T(8,128)(2,1)} %get-tuple-element.52), channel_id=1, source_target_pairs={{0,20},{2,22},{4,16},{5,29},{6,18},{7,31},{8,4},{9,17},{10,6},{11,... | collective-permute-start | bytes 393224 | tf_op jit(solution)/shard_map/ppermute | solution.py:472
  16.9 2.5 %collective-permute-start.5 = (bf16[4,128,128]{2,1,0:T(8,128)(2,1)}, bf16[4,128,128]{2,1,0:T(8,128)(2,1)S(1)}, u32[]{:S(2)}, u32[]{:S(2)}) collective-permute-start(bf16[4,128,128]{2,1,0:T(8,128)(2,1)} %get-tuple-element.55), channel_id=1, source_target_pairs={{0,16},{2,18},{4,8},{5,1},{6,10},{7,3},{9,5},{11,7},{13,25},{15,27... | collective-permute-start | bytes 393224 | tf_op jit(solution)/shard_map/ppermute | solution.py:472
  19.3 1.3 %collective-permute-start.4 = (bf16[4,128,128]{2,1,0:T(8,128)(2,1)}, bf16[4,128,128]{2,1,0:T(8,128)(2,1)S(1)}, u32[]{:S(2)}, u32[]{:S(2)}) collective-permute-start(bf16[4,128,128]{2,1,0:T(8,128)(2,1)} %get-tuple-element.54), channel_id=1, source_target_pairs={{0,4},{1,25},{2,6},{3,27},{9,1},{11,3},{12,20},{13,5},{14,22},{15,... | collective-permute-start | bytes 393224 | tf_op jit(solution)/shard_map/ppermute | solution.py:472
  20.7 1.3 %collective-permute-start.6 = (bf16[4,128,128]{2,1,0:T(8,128)(2,1)}, bf16[4,128,128]{2,1,0:T(8,128)(2,1)S(1)}, u32[]{:S(2)}, u32[]{:S(2)}) collective-permute-start(bf16[4,128,128]{2,1,0:T(8,128)(2,1)} %get-tuple-element.74), channel_id=1, source_target_pairs={{0,8},{1,5},{2,10},{3,7},{4,12},{6,14},{13,17},{15,19},{17,1},{19,... | collective-permute-start | bytes 393224 | tf_op jit(solution)/shard_map/ppermute | solution.py:472
  22.0 1.6 %products.1 = (f32[8,1024]{1,0:T(8,128)S(1)}, f32[1024,1024]{1,0:T(8,128)S(1)}, f32[1024,1024]{1,0:T(8,128)S(1)}, bf16[1024,128]{1,0:T(8,128)(2,1)S(1)}, bf16[10...) custom-call(bf16[2048,128,128]{2,1,0:T(8,128)(2,1)} %get-tuple-eleme, ...), custom_call_target="tpu_custom_call" | custom-call | flops 209715200 | bytes 8388608 | tf_op jit(solution)/shard_map/products/pallas_call | solution.py:483
  23.7 0.4 join.1
  24.1 1.2 %collective-permute-done.4.refs_0_ = bf16[4,128,128]{2,1,0:T(8,128)(2,1)S(1)} collective-permute-done((bf16[4,128,128]{2,1,0:T(8,128)(2,1)}, bf16[4,128,128]{2,1,0:T(8,128)(2,1)S(1)}, u32[]{:S(2)}, u32[]{:S(2)}) %collective-permute-start.4) | collective-permute-done | bytes 131104 | tf_op jit(solution)/shard_map/ppermute | solution.py:472
  25.3 1.5 %softmax.1 = (f32[1024,1024]{1,0:T(8,128)S(1)}, f32[1024,1024]{1,0:T(8,128)S(1)}, bf16[1024,128]{1,0:T(8,128)(2,1)S(1)}, bf16[1024,128]{1,0:T(8,128)(2,1)S(1)}, ...) custom-call(f32[8,1024]{1,0:T(8,128)S(1)} %get-tuple-element.53.bias, ...), custom_call_target="tpu_custom_call", output_to_operand_aliasing={{0}: (2, {}), {1}: (3, {}), {2}: (4, {}), {3}: (5, {}), {4}... | custom-call | flops 805306368 | bytes 8388608 | tf_op jit(solution)/shard_map/softmax/pallas_call | solution.py:507
  26.8 1.1 %collective-permute-done.6.refs_0_ = bf16[4,128,128]{2,1,0:T(8,128)(2,1)S(1)} collective-permute-done((bf16[4,128,128]{2,1,0:T(8,128)(2,1)}, bf16[4,128,128]{2,1,0:T(8,128)(2,1)S(1)}, u32[]{:S(2)}, u32[]{:S(2)}) %collective-permute-start.6) | collective-permute-done | bytes 131104 | tf_op jit(solution)/shard_map/ppermute | solution.py:472
  27.8 2.5 %finish.1 = (bf16[4,128,128]{2,1,0:T(8,128)(2,1)S(1)}, bf16[4,128,128]{2,1,0:T(8,128)(2,1)S(1)}, bf16[4,128,128]{2,1,0:T(8,128)(2,1)S(1)}, bf16[4,128,128]{2,1,0...) custom-call(f32[8,1024]{1,0:T(8,128)S(1)} %get-tuple-element.53.bias, ...), custom_call_target="tpu_custom_call", output_to_operand_aliasing={{8}: (4, {}), {9}: (5, {}), {10}: (6, {}), {11}: (7, {}), {... | custom-call | tf_op jit(solution)/shard_map/finish/pallas_call | solution.py:524
  30.3 3.5 %collective-permute-start.7 = (bf16[4,128,128]{2,1,0:T(8,128)(2,1)S(1)}, bf16[4,128,128]{2,1,0:T(8,128)(2,1)S(1)}, u32[]{:S(2)}, u32[]{:S(2)}) collective-permute-start(bf16[4,128,128]{2,1,0:T(8,128)(2,1)S(1)} %get-tuple-element.85), channel_id=1, source_target_pairs={{12,0},{14,2},{17,5},{19,7},{20,8},{29,9},{22,10},{31,11},{16,12},... | collective-permute-start | bytes 393224 | tf_op jit(solution)/shard_map/ppermute | solution.py:565
  33.8 2.8 %collective-permute-start.8 = (bf16[4,128,128]{2,1,0:T(8,128)(2,1)S(1)}, bf16[4,128,128]{2,1,0:T(8,128)(2,1)S(1)}, u32[]{:S(2)}, u32[]{:S(2)}) collective-permute-start(bf16[4,128,128]{2,1,0:T(8,128)(2,1)S(1)} %get-tuple-element.86), channel_id=1, source_target_pairs={{20,0},{22,2},{16,4},{29,5},{18,6},{31,7},{4,8},{17,9},{6,10},{19,... | collective-permute-start | bytes 393224 | tf_op jit(solution)/shard_map/ppermute | solution.py:565
  36.6 1.9 %collective-permute-start.9 = (bf16[4,128,128]{2,1,0:T(8,128)(2,1)S(1)}, bf16[4,128,128]{2,1,0:T(8,128)(2,1)S(1)}, u32[]{:S(2)}, u32[]{:S(2)}) collective-permute-start(bf16[4,128,128]{2,1,0:T(8,128)(2,1)S(1)} %get-tuple-element.87), channel_id=1, source_target_pairs={{16,0},{18,2},{8,4},{1,5},{10,6},{3,7},{5,9},{7,11},{25,13},{27,15... | collective-permute-start | bytes 393224 | tf_op jit(solution)/shard_map/ppermute | solution.py:565
  38.5 1.3 %collective-permute-start.10 = (bf16[4,128,128]{2,1,0:T(8,128)(2,1)S(1)}, bf16[4,128,128]{2,1,0:T(8,128)(2,1)S(1)}, u32[]{:S(2)}, u32[]{:S(2)}) collective-permute-start(bf16[4,128,128]{2,1,0:T(8,128)(2,1)S(1)} %get-tuple-element.88), channel_id=1, source_target_pairs={{4,0},{25,1},{6,2},{27,3},{1,9},{3,11},{20,12},{5,13},{22,14},{7,1... | collective-permute-start | bytes 393224 | tf_op jit(solution)/shard_map/ppermute | solution.py:565
  39.8 4.0 %collective-permute-start.11 = (bf16[4,128,128]{2,1,0:T(8,128)(2,1)S(1)}, bf16[4,128,128]{2,1,0:T(8,128)(2,1)S(1)}, u32[]{:S(2)}, u32[]{:S(2)}) collective-permute-start(bf16[4,128,128]{2,1,0:T(8,128)(2,1)S(1)} %get-tuple-element.89), channel_id=1, source_target_pairs={{8,0},{5,1},{10,2},{7,3},{12,4},{14,6},{17,13},{19,15},{1,17},{3,1... | collective-permute-start | bytes 393224 | tf_op jit(solution)/shard_map/ppermute | solution.py:565
  43.8 4.9 %collective-permute-start.12 = (bf16[4,128,128]{2,1,0:T(8,128)(2,1)S(1)}, bf16[4,128,128]{2,1,0:T(8,128)(2,1)S(1)}, u32[]{:S(2)}, u32[]{:S(2)}) collective-permute-start(bf16[4,128,128]{2,1,0:T(8,128)(2,1)S(1)} %get-tuple-element.90), channel_id=1, source_target_pairs={{17,1},{19,3},{20,4},{22,6},{12,8},{25,9},{14,10},{27,11},{8,12},{... | collective-permute-start | bytes 393224 | tf_op jit(solution)/shard_map/ppermute | solution.py:565
  48.7 1.9 %collective-permute-start.13 = (bf16[4,128,128]{2,1,0:T(8,128)(2,1)S(1)}, bf16[4,128,128]{2,1,0:T(8,128)(2,1)S(1)}, u32[]{:S(2)}, u32[]{:S(2)}) collective-permute-start(bf16[4,128,128]{2,1,0:T(8,128)(2,1)S(1)} %get-tuple-element.91), channel_id=1, source_target_pairs={{29,1},{31,3},{25,5},{27,7},{16,8},{18,10},{4,12},{6,14},{12,16},{... | collective-permute-start | bytes 393224 | tf_op jit(solution)/shard_map/ppermute | solution.py:565
  50.7 0.8 %collective-permute-done.12.refs_6_ = bf16[4,128,128]{2,1,0:T(8,128)(2,1)S(1)} collective-permute-done((bf16[4,128,128]{2,1,0:T(8,128)(2,1)S(1)}, bf16[4,128,128]{2,1,0:T(8,128)(2,1)S(1)}, u32[]{:S(2)}, u32[]{:S(2)}) %collective-permute-start.12) | collective-permute-done | bytes 131104 | tf_op jit(solution)/shard_map/ppermute | solution.py:565
  51.5 5.6 %collective-permute-done.13.refs_7_ = bf16[4,128,128]{2,1,0:T(8,128)(2,1)S(1)} collective-permute-done((bf16[4,128,128]{2,1,0:T(8,128)(2,1)S(1)}, bf16[4,128,128]{2,1,0:T(8,128)(2,1)S(1)}, u32[]{:S(2)}, u32[]{:S(2)}) %collective-permute-start.13) | collective-permute-done | bytes 131104 | tf_op jit(solution)/shard_map/ppermute | solution.py:565
  57.1 1.2 %unpack.1 = (bf16[128,640]{1,0:T(8,128)(2,1)}, bf16[128,640]{1,0:T(8,128)(2,1)}, bf16[128,640]{1,0:T(8,128)(2,1)}, bf16[128,640]{1,0:T(8,128)(2,1)}) custom-call(bf16[4,128,128]{2,1,0:T(8,128)(2,1)S(1)} %get-tuple-element.84.refs_0_, bf16[4,128,128]{2,1,0:T(8,128)(2,1)S(1)} %collective-permute-done.7.refs_1_, ...), custom_call_target="tpu_custom_call" | custom-call | tf_op jit(solution)/shard_map/unpack/pallas_call | solution.py:567
  (10 shorter events, 0.1 us)
Async XLA Ops:
  3.7 15.7 %collective-permute-start = (bf16[4,128,128]{2,1,0:T(8,128)(2,1)}, bf16[4,128,128]{2,1,0:T(8,128)(2,1)S(1)}, u32[]{:S(2)}, u32[]{:S(2)}) collective-permute-start(bf16[4,128,128]{2,1,0:T(8,128)(2,1)} %get-tuple-element.49), channel_id=1, source_target_pairs={{1,17},{3,19},{4,20},{6,22},{8,12},{9,25},{10,14},{11,27},{12,8},{... | collective-permute-start | bytes 393224 | tf_op jit(solution)/shard_map/ppermute | solution.py:472
  5.0 15.7 %collective-permute-start.1 = (bf16[4,128,128]{2,1,0:T(8,128)(2,1)}, bf16[4,128,128]{2,1,0:T(8,128)(2,1)S(1)}, u32[]{:S(2)}, u32[]{:S(2)}) collective-permute-start(bf16[4,128,128]{2,1,0:T(8,128)(2,1)} %get-tuple-element.50), channel_id=1, source_target_pairs={{0,12},{2,14},{5,17},{7,19},{8,20},{9,29},{10,22},{11,31},{12,16},... | collective-permute-start | bytes 393224 | tf_op jit(solution)/shard_map/ppermute | solution.py:472
  9.1 12.8 %collective-permute-start.2 = (bf16[4,128,128]{2,1,0:T(8,128)(2,1)}, bf16[4,128,128]{2,1,0:T(8,128)(2,1)S(1)}, u32[]{:S(2)}, u32[]{:S(2)}) collective-permute-start(bf16[4,128,128]{2,1,0:T(8,128)(2,1)} %get-tuple-element.51), channel_id=1, source_target_pairs={{1,29},{3,31},{5,25},{7,27},{8,16},{10,18},{12,4},{14,6},{16,12},{... | collective-permute-start | bytes 393224 | tf_op jit(solution)/shard_map/ppermute | solution.py:472
  13.0 9.0 %collective-permute-start.3 = (bf16[4,128,128]{2,1,0:T(8,128)(2,1)}, bf16[4,128,128]{2,1,0:T(8,128)(2,1)S(1)}, u32[]{:S(2)}, u32[]{:S(2)}) collective-permute-start(bf16[4,128,128]{2,1,0:T(8,128)(2,1)} %get-tuple-element.52), channel_id=1, source_target_pairs={{0,20},{2,22},{4,16},{5,29},{6,18},{7,31},{8,4},{9,17},{10,6},{11,... | collective-permute-start | bytes 393224 | tf_op jit(solution)/shard_map/ppermute | solution.py:472
  16.9 6.8 %collective-permute-start.5 = (bf16[4,128,128]{2,1,0:T(8,128)(2,1)}, bf16[4,128,128]{2,1,0:T(8,128)(2,1)S(1)}, u32[]{:S(2)}, u32[]{:S(2)}) collective-permute-start(bf16[4,128,128]{2,1,0:T(8,128)(2,1)} %get-tuple-element.55), channel_id=1, source_target_pairs={{0,16},{2,18},{4,8},{5,1},{6,10},{7,3},{9,5},{11,7},{13,25},{15,27... | collective-permute-start | bytes 393224 | tf_op jit(solution)/shard_map/ppermute | solution.py:472
  19.3 5.9 %collective-permute-start.4 = (bf16[4,128,128]{2,1,0:T(8,128)(2,1)}, bf16[4,128,128]{2,1,0:T(8,128)(2,1)S(1)}, u32[]{:S(2)}, u32[]{:S(2)}) collective-permute-start(bf16[4,128,128]{2,1,0:T(8,128)(2,1)} %get-tuple-element.54), channel_id=1, source_target_pairs={{0,4},{1,25},{2,6},{3,27},{9,1},{11,3},{12,20},{13,5},{14,22},{15,... | collective-permute-start | bytes 393224 | tf_op jit(solution)/shard_map/ppermute | solution.py:472
  20.7 7.2 %collective-permute-start.6 = (bf16[4,128,128]{2,1,0:T(8,128)(2,1)}, bf16[4,128,128]{2,1,0:T(8,128)(2,1)S(1)}, u32[]{:S(2)}, u32[]{:S(2)}) collective-permute-start(bf16[4,128,128]{2,1,0:T(8,128)(2,1)} %get-tuple-element.74), channel_id=1, source_target_pairs={{0,8},{1,5},{2,10},{3,7},{4,12},{6,14},{13,17},{15,19},{17,1},{19,... | collective-permute-start | bytes 393224 | tf_op jit(solution)/shard_map/ppermute | solution.py:472
  30.3 13.5 %collective-permute-start.7 = (bf16[4,128,128]{2,1,0:T(8,128)(2,1)S(1)}, bf16[4,128,128]{2,1,0:T(8,128)(2,1)S(1)}, u32[]{:S(2)}, u32[]{:S(2)}) collective-permute-start(bf16[4,128,128]{2,1,0:T(8,128)(2,1)S(1)} %get-tuple-element.85), channel_id=1, source_target_pairs={{12,0},{14,2},{17,5},{19,7},{20,8},{29,9},{22,10},{31,11},{16,12},... | collective-permute-start | bytes 393224 | tf_op jit(solution)/shard_map/ppermute | solution.py:565
  33.8 14.9 %collective-permute-start.8 = (bf16[4,128,128]{2,1,0:T(8,128)(2,1)S(1)}, bf16[4,128,128]{2,1,0:T(8,128)(2,1)S(1)}, u32[]{:S(2)}, u32[]{:S(2)}) collective-permute-start(bf16[4,128,128]{2,1,0:T(8,128)(2,1)S(1)} %get-tuple-element.86), channel_id=1, source_target_pairs={{20,0},{22,2},{16,4},{29,5},{18,6},{31,7},{4,8},{17,9},{6,10},{19,... | collective-permute-start | bytes 393224 | tf_op jit(solution)/shard_map/ppermute | solution.py:565
  36.6 14.1 %collective-permute-start.9 = (bf16[4,128,128]{2,1,0:T(8,128)(2,1)S(1)}, bf16[4,128,128]{2,1,0:T(8,128)(2,1)S(1)}, u32[]{:S(2)}, u32[]{:S(2)}) collective-permute-start(bf16[4,128,128]{2,1,0:T(8,128)(2,1)S(1)} %get-tuple-element.87), channel_id=1, source_target_pairs={{16,0},{18,2},{8,4},{1,5},{10,6},{3,7},{5,9},{7,11},{25,13},{27,15... | collective-permute-start | bytes 393224 | tf_op jit(solution)/shard_map/ppermute | solution.py:565
  38.5 12.2 %collective-permute-start.10 = (bf16[4,128,128]{2,1,0:T(8,128)(2,1)S(1)}, bf16[4,128,128]{2,1,0:T(8,128)(2,1)S(1)}, u32[]{:S(2)}, u32[]{:S(2)}) collective-permute-start(bf16[4,128,128]{2,1,0:T(8,128)(2,1)S(1)} %get-tuple-element.88), channel_id=1, source_target_pairs={{4,0},{25,1},{6,2},{27,3},{1,9},{3,11},{20,12},{5,13},{22,14},{7,1... | collective-permute-start | bytes 393224 | tf_op jit(solution)/shard_map/ppermute | solution.py:565
  39.8 10.9 %collective-permute-start.11 = (bf16[4,128,128]{2,1,0:T(8,128)(2,1)S(1)}, bf16[4,128,128]{2,1,0:T(8,128)(2,1)S(1)}, u32[]{:S(2)}, u32[]{:S(2)}) collective-permute-start(bf16[4,128,128]{2,1,0:T(8,128)(2,1)S(1)} %get-tuple-element.89), channel_id=1, source_target_pairs={{8,0},{5,1},{10,2},{7,3},{12,4},{14,6},{17,13},{19,15},{1,17},{3,1... | collective-permute-start | bytes 393224 | tf_op jit(solution)/shard_map/ppermute | solution.py:565
  43.8 7.7 %collective-permute-start.12 = (bf16[4,128,128]{2,1,0:T(8,128)(2,1)S(1)}, bf16[4,128,128]{2,1,0:T(8,128)(2,1)S(1)}, u32[]{:S(2)}, u32[]{:S(2)}) collective-permute-start(bf16[4,128,128]{2,1,0:T(8,128)(2,1)S(1)} %get-tuple-element.90), channel_id=1, source_target_pairs={{17,1},{19,3},{20,4},{22,6},{12,8},{25,9},{14,10},{27,11},{8,12},{... | collective-permute-start | bytes 393224 | tf_op jit(solution)/shard_map/ppermute | solution.py:565
  48.7 8.4 %collective-permute-start.13 = (bf16[4,128,128]{2,1,0:T(8,128)(2,1)S(1)}, bf16[4,128,128]{2,1,0:T(8,128)(2,1)S(1)}, u32[]{:S(2)}, u32[]{:S(2)}) collective-permute-start(bf16[4,128,128]{2,1,0:T(8,128)(2,1)S(1)} %get-tuple-element.91), channel_id=1, source_target_pairs={{29,1},{31,3},{25,5},{27,7},{16,8},{18,10},{4,12},{6,14},{12,16},{... | collective-permute-start | bytes 393224 | tf_op jit(solution)/shard_map/ppermute | solution.py:565
